TPU v7x, 32 devices: a whole 2x2x4 slice. The times are simulated.
32 devices in a mesh: groups: 1, rows: 16 (over z, y, core), heads: 2 (over x).
Axes of the slice: x: 2, y: 2, z: 4, core: 2. Of those that a mesh axis runs over, the one named last changes fastest.
Arguments:
- queries: bfloat16 [2048, 8192], P(('groups', 'rows'), 'heads'), may hold values from -40 to 40
- passages: bfloat16 [768, 1024], P(('groups', 'rows')), may hold values from -6 to 6
- enc_gain: bfloat16 [1024], replicated, may hold values from 0.099609375 to 1.8984375
- key_weight: bfloat16 [1024, 8192], P(None, 'heads'), may hold values from -0.1875 to 0.1875
- value_weight: bfloat16 [1024, 8192], P(None, 'heads'), may hold values from -0.1875 to 0.1875
- out_weight: bfloat16 [8192, 1024], P('heads'), may hold values from -0.125 to 0.125
- passage_length: int32 [3], P('groups'), may hold values from 64 to 256, as said below
Outputs:
- cross_out: bfloat16 [2048, 1024], P(('groups', 'rows'))
Inputs may be any that keep to these rules, and one draw needn't show every extreme that they name: `passage_length`: every passage has at least a quarter of its padded tokens; some passage is full and some has exactly 64 tokens.
All inputs are finite; a program needn't handle non-finite values.
Results may differ from a plain program's by a relative error of at most 0.012.
The roundings to bfloat16 on the way count: a program that leaves them out, or rounds other values in their place, can miss the bound.
Values may be sent and summed in bfloat16 or wider, within the bound.
No kernel may reach another device: no remote copies, remote signals or barrier semaphores. Data moves between devices by JAX's collectives and lax.ppermute only.
A program may use at most 128 MiB of HBM per device.

v0:
```python
import jax
import jax.numpy as jnp
from jax import lax
from jax.sharding import PartitionSpec as P

DK = 128
PASS_LEN = 256


LOWEST = -1e30


def normalize(rows_in, enc_gain):
    wide = rows_in.astype(jnp.float32)
    mean_square = jnp.mean(wide * wide, axis=-1, keepdims=True)
    return (wide * lax.rsqrt(mean_square + 1e-06) * enc_gain.astype(jnp.float32)).astype(
        jnp.bfloat16
    )


def project(rows_in, enc_gain, key_weight, value_weight):
    normed = normalize(rows_in, enc_gain)
    key_rows = jnp.dot(normed, key_weight, preferred_element_type=jnp.float32).astype(jnp.bfloat16)
    value_rows = jnp.dot(normed, value_weight, preferred_element_type=jnp.float32).astype(
        jnp.bfloat16
    )
    return (key_rows, value_rows)


def row_mask(passage_length, number):
    positions = jnp.arange(number, dtype=jnp.int32)
    owner = positions // PASS_LEN
    offset = positions % PASS_LEN
    matches = owner[:, None] == jnp.arange(passage_length.shape[0], dtype=jnp.int32)[None, :]
    row_length = jnp.sum(jnp.where(matches, passage_length[None, :], 0), axis=1)
    return offset < row_length


def attend(carry, query_heads, key_rows, value_rows, passage_length):
    best, denom, summed = carry
    number = key_rows.shape[0]
    heads_here = query_heads.shape[1]
    key_heads = key_rows.reshape(number, heads_here, DK)
    value_heads = value_rows.reshape(number, heads_here, DK)
    scores = jnp.einsum("thd,ehd->hte", query_heads, key_heads, preferred_element_type=jnp.float32)
    valid = row_mask(passage_length, number)[None, None, :]
    masked = jnp.where(valid, scores, LOWEST)
    new_best = jnp.maximum(best, jnp.max(masked, axis=-1))
    expo = jnp.where(valid, jnp.exp(scores - new_best[:, :, None]), 0.0)
    factor = jnp.exp(best - new_best)
    denom = jnp.sum(expo, axis=-1)
    mixed = jnp.einsum(
        "hte,ehd->thd", expo.astype(jnp.bfloat16), value_heads, preferred_element_type=jnp.float32
    )
    summed = summed * factor.T[:, :, None] + mixed
    return (new_best, denom, summed)


def on_device(queries, passages, enc_gain, key_weight, value_weight, out_weight, passage_length):
    rows_here = queries.shape[0]
    inner = queries.shape[1]
    heads_here = inner // DK
    query_heads = queries.reshape(rows_here, heads_here, DK)
    start_carry = (
        jnp.full((heads_here, rows_here), LOWEST, jnp.float32),
        jnp.zeros((heads_here, rows_here), jnp.float32),
        jnp.zeros((rows_here, heads_here, DK), jnp.float32),
    )
    key_rows, value_rows = project(
        lax.all_gather(passages, "rows", axis=0, tiled=True), enc_gain, key_weight, value_weight
    )
    best, denom, summed = attend(start_carry, query_heads, key_rows, value_rows, passage_length)
    attended = (summed / denom.T[:, :, None]).astype(jnp.bfloat16).reshape(rows_here, inner)
    partial_out = jnp.dot(attended, out_weight, preferred_element_type=jnp.float32)
    share = lax.psum_scatter(
        partial_out.astype(jnp.bfloat16), "heads", scatter_dimension=1, tiled=True
    )
    cross_out = lax.all_gather(share, "heads", axis=1, tiled=True)
    return cross_out


def solution(mesh):
    return jax.shard_map(
        on_device,
        mesh=mesh,
        in_specs=(
            P(("groups", "rows"), "heads"),
            P(("groups", "rows"), None),
            P(),
            P(None, "heads"),
            P(None, "heads"),
            P("heads", None),
            P("groups"),
        ),
        out_specs=P(("groups", "rows"), None),
        check_vma=False,
    )
```

profile of v0, /device:TPU:0, one launch (start us, length us, event | category | flops | bytes accessed | tf_op | source)
XLA Modules:
  0.0 132.8 jit_solution(18445588045736639414)
XLA Ops:
  6.5 0.0 copy-start
  6.5 0.0 all-gather.2.cloned.1.call-start
  6.5 0.7 all-gather.2.cloned.1.call-update
  7.3 0.0 reduce-scatter.2.cloned.1.call-start
  7.3 0.7 convert_element_type.25
  8.0 0.7 select_reduce_fusion.1
  8.7 43.3 %all-gather.2.cloned.1.call-done = bf16[768,1024]{1,0:T(8,128)(2,1)} async-done(((bf16[48,1024]{1,0:T(8,128)(2,1)}), bf16[768,1024]{1,0:T(8,128)(2,1)}) %all-gather.2.cloned.1.call-update) | async-done | bytes 1572880 | tf_op jit(solution)/shard_map/all_gather | solution.py:70
  52.0 1.8 %fusion.7 = f32[768]{0:T(1024)S(1)} fusion(bf16[768,1024]{1,0:T(8,128)(2,1)} %all-gather.2.cloned.1.call-done), kind=kLoop, calls=%fused_computation.15 | loop fusion | flops 2358528 | bytes 1575936 | tf_op jit(solution)/shard_map/reduce_sum | solution.py:15
  53.8 12.5 %convolution_convert_fusion = bf16[768,4096]{1,0:T(8,128)(2,1)} fusion(bf16[1024,4096]{1,0:T(8,128)(2,1)} %param.11, bf16[768,1024]{1,0:T(8,128)(2,1)} %all-gather.2.cloned.1.call-done, f32[1024]{0:T(1024)S(1)} %convert_element_type.25, f32[768]{0:T(1024)S(1)} %add_rsqrt_fusion), kind=kOutput, calls=%fused_computation.4 | convolution fusion | flops 6448742400 | bytes 16260096 | tf_op jit(solution)/shard_map/dot_general | solution.py:24
  66.3 0.0 copy-start.2
  66.3 8.8 %copy.17 = bf16[768,4096]{0,1:T(8,128)(2,1)} copy(bf16[768,4096]{1,0:T(8,128)(2,1)} %convolution_convert_fusion) | data formatting | bytes 12582912 | tf_op jit(solution)/shard_map/reshape | solution.py:44
  75.1 0.0 copy-done.2
  75.1 12.2 %fusion.10 = bf16[96,32,8,128]{3,2,1,0:T(8,128)(2,1)} fusion(bf16[1024,4096]{1,0:T(8,128)(2,1)} %param.10, bf16[768,1024]{1,0:T(8,128)(2,1)S(1)} %copy-done.2, f32[1024]{0:T(1024)S(1)} %convert_element_type.25, f32[768]{0:T(1024)S(1)} %add_rsqrt_fusion), kind=kOutput, calls=%fused_computation.18 | convolution fusion | flops 6448742400 | bytes 16260096 | tf_op jit(solution)/shard_map/dot_general | solution.py:23
  87.3 0.0 copy-done
  87.3 4.2 %select_reduce_fusion = (f32[32,128]{1,0:T(8,128)S(1)}, f32[32,768,128]{2,1,0:T(8,128)S(1)}) fusion(pred[768]{0:T(1024)(128)(4,1)S(1)} %fusion.17, bf16[96,32,8,128]{3,2,1,0:T(8,128)(2,1)} %fusion.10, bf16[128,4096]{1,0:T(8,128)(2,1)S(1)} %copy-done), kind=kOutput, calls=%fused_computation.3 | convolution fusion | flops 811593728 | bytes 19940096 | tf_op jit(solution)/shard_map/thd,ehd->hte/dot_general | solution.py:45
  91.5 0.0 copy-start.1
  91.6 0.0 slice-start
  91.6 2.9 %bitcast_reduce_fusion = f32[32,128]{1,0:T(8,128)S(1)} fusion(f32[32,768,128]{2,1,0:T(8,128)S(1)} %get-tuple-element.8, f32[32,128]{1,0:T(8,128)S(1)} %get-tuple-element.6, pred[768]{0:T(1024)(128)(4,1)S(1)} %fusion.17), kind=kLoop, calls=%fused_computation | loop fusion | flops 9433088 | bytes 12616448 | tf_op jit(solution)/shard_map/reduce_sum | solution.py:51
  94.5 2.7 %copy-done.1 = f32[32,768,128]{2,1,0:T(8,128)} copy-done((f32[32,768,128]{2,1,0:T(8,128)}, f32[32,768,128]{2,1,0:T(8,128)S(1)}, u32[]{:S(2)}) %copy-start.1) | copy-done | bytes 12582936
  97.2 0.0 slice-start.1
  97.2 9.2 %fusion.12 = bf16[128,32,128]{0,2,1:T(8,128)(2,1)S(1)} fusion(bf16[768,32,128]{0,2,1:T(8,128)(2,1)} %bitcast.40, f32[32,768,128]{2,1,0:T(8,128)} %copy-done.1, f32[32,128]{1,0:T(8,128)S(1)} %get-tuple-element.6, pred[768]{0:T(1024)(128)(4,1)S(1)} %fusion.17, f32[128,32]{0,1:T(8,128)S(1)} %bitcast.42, f32[128,32]{0,1:T(8,128)S(1)} %get-tuple-element.5), kind=kOutput, calls=%fused_computation.21 | convolution fusion | flops 816316416 | bytes 19972864 | tf_op jit(solution)/shard_map/hte,ehd->thd/dot_general | solution.py:52
  106.4 0.0 slice-done
  106.5 0.0 slice-done.1
  106.5 2.0 %convolution_convert_fusion.2 = bf16[128,1024]{1,0:T(8,128)(2,1)} fusion(bf16[128,4096]{0,1:T(8,128)(2,1)S(1)} %bitcast.41, bf16[4096,1024]{1,0:T(8,128)(2,1)S(1)} %bitcast.39), kind=kOutput, calls=%fused_computation.22 | convolution fusion | flops 1073872896 | bytes 9699328 | tf_op jit(solution)/shard_map/dot_general | solution.py:74
  108.5 0.0 reduce-scatter.2.cloned.1.call-update
  108.5 10.7 %reduce-scatter.2.cloned.1.call-done = bf16[128,512]{1,0:T(8,128)(2,1)} async-done(((bf16[128,1024]{1,0:T(8,128)(2,1)}), bf16[128,512]{1,0:T(8,128)(2,1)}) %reduce-scatter.2.cloned.1.call-update) | async-done | bytes 131088 | tf_op jit(solution)/shard_map/reduce_scatter | solution.py:75
  119.2 6.1 %all_gather.7 = bf16[128,1024]{1,0:T(8,128)(2,1)S(1)} all-gather(bf16[128,512]{1,0:T(8,128)(2,1)} %reduce-scatter.2.cloned.1.call-done), channel_id=1, replica_groups=mesh['groups'=1,'rows'=16,'heads'=2] {'heads'}, dimensions={1}, use_global_device_ids=true | all-gather | bytes 393216 | tf_op jit(solution)/shard_map/all_gather | solution.py:78
  125.3 0.7 copy.33
  (5 shorter events, 0.0 us)
Async XLA Ops:
  6.5 80.8 %copy-start = (bf16[128,4096]{1,0:T(8,128)(2,1)S(1)}, bf16[128,4096]{1,0:T(8,128)(2,1)}, u32[]{:S(2)}) copy-start(bf16[128,4096]{1,0:T(8,128)(2,1)} %param.7) | copy-start | bytes 3145732
  6.5 45.5 %all-gather.2.cloned.1.call-start = ((), (), s32[]{:S(2)}) async-start(), calls=%async_computation.1 | async-start | bytes 1671168 | tf_op jit(solution)/shard_map/all_gather | solution.py:70
  7.3 111.9 %reduce-scatter.2.cloned.1.call-start = ((), (), s32[]{:S(2)}) async-start(), calls=%async_computation.2 | async-start | bytes 393216 | tf_op jit(solution)/shard_map/reduce_scatter | solution.py:75
  66.3 8.8 %copy-start.2 = (bf16[768,1024]{1,0:T(8,128)(2,1)S(1)}, bf16[768,1024]{1,0:T(8,128)(2,1)}, u32[]{:S(2)}) copy-start(bf16[768,1024]{1,0:T(8,128)(2,1)} %all-gather.2.cloned.1.call-done) | copy-start | bytes 4718596
  91.5 5.7 %copy-start.1 = (f32[32,768,128]{2,1,0:T(8,128)}, f32[32,768,128]{2,1,0:T(8,128)S(1)}, u32[]{:S(2)}) copy-start(f32[32,768,128]{2,1,0:T(8,128)S(1)} %get-tuple-element.8) | copy-start | bytes 37748740
  91.6 14.9 %slice-start = ((s8[8388608]{0:T(1024)(128)(4,1)}), s8[4194304]{0:T(1024)(128)(4,1)S(1)}, s32[]{:S(2)}) async-start(s8[8388608]{0:T(1024)(128)(4,1)} %bitcast.38), calls=%async_computation.3 | async-start | bytes 8388608
  97.2 9.2 %slice-start.1 = ((s8[8388608]{0:T(1024)(128)(4,1)}), s8[4194304]{0:T(1024)(128)(4,1)S(1)}, s32[]{:S(2)}) async-start(s8[8388608]{0:T(1024)(128)(4,1)} %bitcast.38), calls=%async_computation.4 | async-start | bytes 8388608
Sparse Core Ops, SparseCore 0:
  9.6 42.3 all-gather.1
  108.6 10.5 reduce-scatter.1
where the time goes:
time: 133 us
  waiting for transfers between devices  54.7 us (41%)
  matrix products  40 us (30%)
  between operations  13.5 us (10%)
  local copies, waits for them, and re-layouts  12.3 us (9%)
  other arithmetic  6.14 us (5%)
  blocking collectives  6.12 us (5%)
    all_gather x1, waiting for transfers between devices, on_device(): lax.all_gather(passages, 'rows', axis=0, tiled=True)  43.3 us
    dot_general x1, matrix products, project(): jnp.dot(normed, value_weight, preferred_element_type=jnp.float32)  12.5 us
    dot_general x1, matrix products, project(): jnp.dot(normed, key_weight, preferred_element_type=jnp.float32)  12.2 us
    reduce_scatter x1, waiting for transfers between devices, on_device(): lax.psum_scatter(partial_out.astype(jnp.bfloat16), 'heads', scatter_dimen...  10.7 us
    dot_general x1, matrix products, attend(): jnp.einsum('hte,ehd->thd', expo.astype(jnp.bfloat16), value_heads, prefer...  9.19 us
    reshape x1, local copies, waits for them, and re-layouts, attend(): value_heads = value_rows.reshape(number, heads_here, DK)  8.82 us
    all_gather x1, blocking collectives, on_device(): cross_out = lax.all_gather(share, 'heads', axis=1, tiled=True)  6.12 us
    dot_general x1, matrix products, attend(): jnp.einsum('thd,ehd->hte', query_heads, key_heads, preferred_element_type...  4.22 us
  transfers between devices with their start and end apart: 2, of which 2 were waited for; matrix products, arithmetic and copies ran while one was open for 1% of the time, Pallas kernels for 0%

commit v1 on v0

v1 whole, which is shorter than its diff:
```python
import functools

import jax
import jax.numpy as jnp
from jax import lax
from jax.experimental import pallas as pl
from jax.experimental.pallas import tpu as pltpu
from jax.sharding import PartitionSpec as P

DK = 128
PASS_LEN = 256
LOWEST = -1e30
TILE = 16
HEADS_STEP = 2


def chip_cycle(chips):
    up = list(range(0, chips, 2))
    return up + [chip for chip in range(chips - 1, -1, -1) if chip % 2]


def gather_pieces(passages, number):
    chips = number // 2
    cycle = chip_cycle(chips)
    place = {chip: index for index, chip in enumerate(cycle)}

    def hop(by):
        return [
            (2 * chip + core, 2 * cycle[(place[chip] + by) % chips] + core)
            for chip in range(chips)
            for core in range(2)
        ]

    other_core = [(device, device ^ 1) for device in range(number)]
    pieces, offsets = [passages], [0]
    ahead = behind = passages
    for step in range(1, chips // 2 + 1):
        ahead = lax.ppermute(ahead, "rows", hop(1))
        pieces.append(ahead)
        offsets.append(-step)
        if 2 * step < chips:
            behind = lax.ppermute(behind, "rows", hop(-1))
            pieces.append(behind)
            offsets.append(step)
    swapped = [lax.ppermute(piece, "rows", other_core) for piece in pieces]
    owners = []
    for device in range(number):
        at, core = place[device // 2], device % 2
        from_chips = [cycle[(at + offset) % chips] for offset in offsets]
        owners.append(
            [2 * chip + core for chip in from_chips]
            + [2 * chip + 1 - core for chip in from_chips]
        )
    return pieces + swapped, owners


def kernel(cases, device_ref, length_ref, owners_ref, *refs):
    piece_refs = refs[: owners_ref.shape[1]]
    (gain_ref, own_q_ref, other_q_ref, key_ref, value_ref, out_w_ref,
     own_ref, other_ref, normed, bias, total, count, partial) = refs[owners_ref.shape[1]:]
    step = pl.program_id(0)
    rows_piece = piece_refs[0].shape[0]
    passages = length_ref.shape[0]

    @pl.when(step == 0)
    def _():
        total[...] = jnp.zeros_like(total)
        normed[...] = jnp.zeros_like(normed)
        for passage in range(passages):
            partial[passage] = -1
        device = device_ref[0]
        gain = gain_ref[...].astype(jnp.float32)
        kept = jnp.int32(0)
        for index, piece_ref in enumerate(piece_refs):
            first = owners_ref[device, index] * rows_piece
            for tile in range(rows_piece // TILE):
                row = first + tile * TILE
                passage = row // PASS_LEN
                here = length_ref[passage] - row % PASS_LEN

                @pl.when(here > 0)
                def _(kept=kept, tile=tile, piece_ref=piece_ref, here=here, passage=passage):
                    wide = piece_ref[tile * TILE:(tile + 1) * TILE, :].astype(jnp.float32)
                    mean_square = jnp.mean(wide * wide, axis=-1, keepdims=True)
                    scaled = wide * lax.rsqrt(mean_square + 1e-06) * gain
                    at = pl.multiple_of(kept * TILE, TILE)
                    normed[pl.ds(at, TILE), :] = scaled.astype(jnp.bfloat16)

                    @pl.when(here < TILE)
                    def _():
                        partial[passage] = kept * TILE + here

                kept = kept + (here > 0).astype(jnp.int32)
        count[0] = kept * TILE
        lane = lax.broadcasted_iota(jnp.int32, bias.shape, 1)
        valid = lane < kept * TILE
        for passage in range(passages):
            begin = partial[passage]
            end = (begin + TILE - 1) // TILE * TILE
            valid = valid & ((begin < 0) | (lane < begin) | (lane >= end))
        bias[...] = jnp.where(valid, 0.0, LOWEST)

    def attend(number):
        rows_in = normed[:number, :]
        key_rows = jnp.dot(
            rows_in, key_ref[...], preferred_element_type=jnp.float32
        ).astype(jnp.bfloat16)
        value_rows = jnp.dot(
            rows_in, value_ref[...], preferred_element_type=jnp.float32
        ).astype(jnp.bfloat16)
        query_rows = jnp.concatenate([own_q_ref[...], other_q_ref[...]], axis=0)
        shift = bias[0:1, :number]
        attended = []
        for head in range(HEADS_STEP):
            columns = slice(head * DK, (head + 1) * DK)
            scores = lax.dot_general(
                query_rows[:, columns], key_rows[:, columns],
                (((1,), (1,)), ((), ())), preferred_element_type=jnp.float32,
            ) + shift
            top = jnp.max(scores, axis=-1, keepdims=True)
            expo = jnp.exp(scores - top)
            denom = jnp.sum(expo, axis=-1, keepdims=True)
            mixed = jnp.dot(
                expo.astype(jnp.bfloat16), value_rows[:, columns],
                preferred_element_type=jnp.float32,
            )
            attended.append((mixed / denom).astype(jnp.bfloat16))
        total[...] += jnp.dot(
            jnp.concatenate(attended, axis=1), out_w_ref[...],
            preferred_element_type=jnp.float32,
        )

    low = 0
    for number in cases:
        pl.when((count[0] > low) & (count[0] <= number))(functools.partial(attend, number))
        low = number

    @pl.when(step == pl.num_programs(0) - 1)
    def _():
        half = own_ref.shape[0]
        own_ref[...] = total[:half, :].astype(jnp.bfloat16)
        other_ref[...] = total[half:, :].astype(jnp.bfloat16)


def on_device(number, queries, passages, enc_gain, key_weight, value_weight, out_weight, passage_length):
    rows_here, inner = queries.shape
    width = passages.shape[1]
    half = inner // 2
    steps = half // (HEADS_STEP * DK)
    block = HEADS_STEP * DK
    enc_rows = passages.shape[0] * number
    device = lax.axis_index("rows")
    core = device % 2
    other_core = [(place, place ^ 1) for place in range(number)]
    heads_axis = lax.axis_size("heads")

    given = lax.dynamic_slice_in_dim(queries, (1 - core) * half, half, axis=1)
    other_queries = lax.ppermute(given, "rows", other_core)
    pieces, owners = gather_pieces(passages, number)

    cases = [enc_rows * part // 12 // 64 * 64 for part in (6, 7, 8, 9)] + [enc_rows]
    whole = lambda shape: pl.BlockSpec(shape, lambda i, *_: (0,) * len(shape))
    own, other = pl.pallas_call(
        functools.partial(kernel, cases),
        grid_spec=pltpu.PrefetchScalarGridSpec(
            num_scalar_prefetch=3,
            grid=(steps,),
            in_specs=[whole(passages.shape)] * len(pieces) + [
                whole((1, width)),
                pl.BlockSpec((rows_here, block), lambda i, d, *_: (0, d[0] % 2 * steps + i)),
                pl.BlockSpec((rows_here, block), lambda i, *_: (0, i)),
                pl.BlockSpec((width, block), lambda i, d, *_: (0, d[0] % 2 * steps + i)),
                pl.BlockSpec((width, block), lambda i, d, *_: (0, d[0] % 2 * steps + i)),
                pl.BlockSpec((block, width), lambda i, d, *_: (d[0] % 2 * steps + i, 0)),
            ],
            out_specs=[whole((rows_here, width))] * 2,
            scratch_shapes=[
                pltpu.VMEM((enc_rows, width), jnp.bfloat16),
                pltpu.VMEM((8, enc_rows), jnp.float32),
                pltpu.VMEM((2 * rows_here, width), jnp.float32),
                pltpu.SMEM((1,), jnp.int32),
                pltpu.SMEM((passage_length.shape[0],), jnp.int32),
            ],
        ),
        out_shape=[jax.ShapeDtypeStruct((rows_here, width), jnp.bfloat16)] * 2,
        compiler_params=pltpu.CompilerParams(vmem_limit_bytes=40 * 1024 * 1024),
        name="attention",
    )(
        device.reshape(1), passage_length, jnp.array(owners, jnp.int32), *pieces,
        enc_gain.reshape(1, width), queries, other_queries, key_weight, value_weight, out_weight,
    )
    received = lax.ppermute(other, "rows", other_core)
    share = (own.astype(jnp.float32) + received.astype(jnp.float32)).astype(jnp.bfloat16)
    by = 1
    while by < heads_axis:
        turn = [(place, place ^ by) for place in range(heads_axis)]
        given = lax.ppermute(share, "heads", turn)
        share = (share.astype(jnp.float32) + given.astype(jnp.float32)).astype(jnp.bfloat16)
        by *= 2
    return share


def solution(mesh):
    return jax.shard_map(
        functools.partial(on_device, mesh.shape["rows"]),
        mesh=mesh,
        in_specs=(
            P(("groups", "rows"), "heads"),
            P(("groups", "rows"), None),
            P(),
            P(None, "heads"),
            P(None, "heads"),
            P("heads", None),
            P("groups"),
        ),
        out_specs=P(("groups", "rows"), None),
        check_vma=False,
    )
```

time: 133 us -> 63.7 us (0.48)
  matrix products: 40 us -> 0 us
  waiting for transfers between devices: 54.7 us -> 19.3 us
  Pallas kernels: 0 us -> 22.7 us
  between operations: 13.5 us -> 0.05 us
  starting transfers between devices: 0.04 us -> 11.9 us
  blocking collectives: 6.12 us -> 0 us
  other arithmetic: 6.14 us -> 0.84 us
  local copies, waits for them, and re-layouts: 12.3 us -> 8.61 us
    all_gather x1 -> x0, waiting for transfers between devices: 43.3 us -> none  [on_device(): lax.all_gather(passages, 'rows', axis=0, tiled=True)]
    dot_general x5 -> x0, matrix products: 40 us -> none  [the longest x1 12.5 us: project(): jnp.dot(normed, value_weight, preferred_element_type=jnp.float32)]
    pallas_call x0 -> x1, Pallas kernels: none -> 22.7 us  [on_device(): pl.pallas_call(functools.partial(kernel, cases), grid_spec=pltpu.Prefetch...]
    ppermute x0 -> x18, waiting for transfers between devices: none -> 19.3 us  [the longest x4 9.45 us: gather_pieces(): ahead = lax.ppermute(ahead, 'rows', hop(1))]
    ppermute x0 -> x18, starting transfers between devices: none -> 11.9 us  [the longest x4 8.04 us: gather_pieces(): ahead = lax.ppermute(ahead, 'rows', hop(1))]
    reduce_scatter x1 -> x0, waiting for transfers between devices: 10.7 us -> none  [on_device(): lax.psum_scatter(partial_out.astype(jnp.bfloat16), 'heads', scatter_dimen...]
    reshape x1, local copies, waits for them, and re-layouts: 8.82 us -> 0.69 us  [on_device(): enc_gain.reshape(1, width)]
    all_gather x1 -> x0, blocking collectives: 6.12 us -> none  [on_device(): cross_out = lax.all_gather(share, 'heads', axis=1, tiled=True)]
  transfers between devices with their start and end apart: 2 -> 18, of which waited for: 2 -> 9; matrix products, arithmetic and copies ran while one was open for 1% -> 1% of each run, Pallas kernels for 0% -> 0%
where the time goes in v1:
time: 63.7 us; the launch traced here: 63.4 us
  Pallas kernels  22.7 us (36%)
  waiting for transfers between devices  19.3 us (30%)
  starting transfers between devices  11.9 us (19%)
  local copies, waits for them, and re-layouts  8.61 us (14%)
  other arithmetic  0.84 us (1%)
    pallas_call x1, Pallas kernels, on_device(): pl.pallas_call(functools.partial(kernel, cases), grid_spec=pltpu.Prefetch...  22.7 us
    ppermute x4, waiting for transfers between devices, gather_pieces(): ahead = lax.ppermute(ahead, 'rows', hop(1))  9.45 us
    ppermute x4, starting transfers between devices, gather_pieces(): ahead = lax.ppermute(ahead, 'rows', hop(1))  8.04 us
    unnamed x10, local copies, waits for them, and re-layouts  6.85 us
    ppermute x1, waiting for transfers between devices, on_device(): given = lax.ppermute(share, 'heads', turn)  6.65 us
    ppermute x1, starting transfers between devices, on_device(): given = lax.ppermute(share, 'heads', turn)  1.78 us
    ppermute x1, waiting for transfers between devices, on_device(): received = lax.ppermute(other, 'rows', other_core)  1.38 us
  transfers between devices with their start and end apart: 18, of which 9 were waited for; matrix products, arithmetic and copies ran while one was open for 1% of the time, Pallas kernels for 0%

profile of v1, /device:TPU:0, one launch (start us, length us, event | category | flops | bytes accessed | tf_op | source)
XLA Modules:
  0.0 63.4 jit_solution(2087267100930649735)
XLA Ops:
  0.0 1.1 %constant_dynamic-slice_fusion = bf16[128,2048]{1,0:T(8,128)(2,1)S(1)} fusion(bf16[128,4096]{1,0:T(8,128)(2,1)} %refs_17_.1, s32[]{:T(128)S(6)} %select_n.11), kind=kLoop, calls=%fused_computation.2 | loop fusion | bytes 1048580 | tf_op jit(solution)/shard_map/dynamic_slice | solution.py:157
  1.1 0.5 collective-permute-start.15
  1.6 2.6 %collective-permute-start = (bf16[48,1024]{1,0:T(8,128)(2,1)}, bf16[48,1024]{1,0:T(8,128)(2,1)S(1)}, u32[]{:S(2)}, u32[]{:S(2)}) collective-permute-start(bf16[48,1024]{1,0:T(8,128)(2,1)} %refs_0_.1), channel_id=1, source_target_pairs={{0,8},{2,10},{4,0},{6,2},{8,16},{10,18},{12,4},{14,6},{16,24},{18,... | collective-permute-start | bytes 294920 | tf_op jit(solution)/shard_map/ppermute | solution.py:38
  4.2 0.0 collective-permute-start.1
  4.3 3.5 %collective-permute-done.refs_1_ = bf16[48,1024]{1,0:T(8,128)(2,1)S(1)} collective-permute-done((bf16[48,1024]{1,0:T(8,128)(2,1)}, bf16[48,1024]{1,0:T(8,128)(2,1)S(1)}, u32[]{:S(2)}, u32[]{:S(2)}) %collective-permute-start) | collective-permute-done | bytes 98336 | tf_op jit(solution)/shard_map/ppermute | solution.py:38
  7.8 1.8 %collective-permute-start.2 = (bf16[48,1024]{1,0:T(8,128)(2,1)S(1)}, bf16[48,1024]{1,0:T(8,128)(2,1)S(1)}, u32[]{:S(2)}, u32[]{:S(2)}) collective-permute-start(bf16[48,1024]{1,0:T(8,128)(2,1)S(1)} %collective-permute-done.refs_1_), channel_id=1, source_target_pairs={{0,8},{2,10},{4,0},{6,2},{8,16},{10,18},{12,4},{14,6},{16,24},{18,... | collective-permute-start | bytes 294920 | tf_op jit(solution)/shard_map/ppermute | solution.py:38
  9.6 0.0 collective-permute-done.1.refs_2_
  9.6 0.2 collective-permute-start.3
  9.8 0.3 collective-permute-start.8
  10.1 2.3 %collective-permute-done.2.refs_3_ = bf16[48,1024]{1,0:T(8,128)(2,1)S(1)} collective-permute-done((bf16[48,1024]{1,0:T(8,128)(2,1)S(1)}, bf16[48,1024]{1,0:T(8,128)(2,1)S(1)}, u32[]{:S(2)}, u32[]{:S(2)}) %collective-permute-start.2) | collective-permute-done | bytes 98336 | tf_op jit(solution)/shard_map/ppermute | solution.py:38
  12.4 1.8 %collective-permute-start.4 = (bf16[48,1024]{1,0:T(8,128)(2,1)S(1)}, bf16[48,1024]{1,0:T(8,128)(2,1)S(1)}, u32[]{:S(2)}, u32[]{:S(2)}) collective-permute-start(bf16[48,1024]{1,0:T(8,128)(2,1)S(1)} %collective-permute-done.2.refs_3_), channel_id=1, source_target_pairs={{0,8},{2,10},{4,0},{6,2},{8,16},{10,18},{12,4},{14,6},{16,24},{18,... | collective-permute-start | bytes 294920 | tf_op jit(solution)/shard_map/ppermute | solution.py:38
  14.2 0.6 collective-permute-done.3.refs_4_
  14.8 0.3 collective-permute-start.5
  15.1 1.9 %collective-permute-done.4.refs_5_ = bf16[48,1024]{1,0:T(8,128)(2,1)S(1)} collective-permute-done((bf16[48,1024]{1,0:T(8,128)(2,1)S(1)}, bf16[48,1024]{1,0:T(8,128)(2,1)S(1)}, u32[]{:S(2)}, u32[]{:S(2)}) %collective-permute-start.4) | collective-permute-done | bytes 98336 | tf_op jit(solution)/shard_map/ppermute | solution.py:38
  17.0 1.8 %collective-permute-start.6 = (bf16[48,1024]{1,0:T(8,128)(2,1)S(1)}, bf16[48,1024]{1,0:T(8,128)(2,1)S(1)}, u32[]{:S(2)}, u32[]{:S(2)}) collective-permute-start(bf16[48,1024]{1,0:T(8,128)(2,1)S(1)} %collective-permute-done.4.refs_5_), channel_id=1, source_target_pairs={{0,8},{2,10},{4,0},{6,2},{8,16},{10,18},{12,4},{14,6},{16,24},{18,... | collective-permute-start | bytes 294920 | tf_op jit(solution)/shard_map/ppermute | solution.py:38
  18.8 0.6 collective-permute-done.5.refs_6_
  19.4 0.5 collective-permute-start.13
  19.9 1.7 %collective-permute-done.6.refs_7_ = bf16[48,1024]{1,0:T(8,128)(2,1)S(1)} collective-permute-done((bf16[48,1024]{1,0:T(8,128)(2,1)S(1)}, bf16[48,1024]{1,0:T(8,128)(2,1)S(1)}, u32[]{:S(2)}, u32[]{:S(2)}) %collective-permute-start.6) | collective-permute-done | bytes 98336 | tf_op jit(solution)/shard_map/ppermute | solution.py:38
  21.6 0.7 %reshape.7.refs_16_ = bf16[1,1024]{1,0:T(2,128)(2,1)S(1)} reshape(bf16[1024]{0:T(1024)(128)(2,1)} %param.10) | data formatting | bytes 4096 | tf_op jit(solution)/shard_map/reshape | solution.py:190
  22.4 0.6 collective-permute-done.14.refs_15_
  22.9 3.4 %copy-done = bf16[1024,4096]{1,0:T(8,128)(2,1)S(1)} copy-done((bf16[1024,4096]{1,0:T(8,128)(2,1)S(1)}, bf16[1024,4096]{1,0:T(8,128)(2,1)}, u32[]{:S(2)}) %copy-start) | copy-done | bytes 8388632
  26.3 1.2 %copy-done.1 = bf16[128,4096]{1,0:T(8,128)(2,1)S(1)} copy-done((bf16[128,4096]{1,0:T(8,128)(2,1)S(1)}, bf16[128,4096]{1,0:T(8,128)(2,1)}, u32[]{:S(2)}) %copy-start.1) | copy-done | bytes 1048600
  27.6 0.9 %copy-done.2 = bf16[48,1024]{1,0:T(8,128)(2,1)S(1)} copy-done((bf16[48,1024]{1,0:T(8,128)(2,1)S(1)}, bf16[48,1024]{1,0:T(8,128)(2,1)}, u32[]{:S(2)}) %copy-start.2) | copy-done | bytes 98328
  28.5 0.7 %copy-done.3 = s32[16,16]{1,0:T(8,128)S(1)} copy-done((s32[16,16]{1,0:T(8,128)S(1)}, s32[16,16]{1,0:T(8,128)}, u32[]{:S(2)}) %copy-start.3) | copy-done | bytes 1048
  29.1 0.7 %copy-done.4 = s32[3]{0:T(128)S(1)} copy-done((s32[3]{0:T(128)S(1)}, s32[3]{0:T(128)}, u32[]{:S(2)}) %copy-start.4) | copy-done | bytes 36
  29.8 22.7 %attention.1 = (bf16[128,1024]{1,0:T(8,128)(2,1)S(1)}, bf16[128,1024]{1,0:T(8,128)(2,1)S(1)}) custom-call(s32[1]{0:T(128)} %bitcast.device_ref, s32[3]{0:T(128)S(1)} %copy-done.4, s32[16,16]{1,0:T(8,128)S(1)} %copy-done.3, bf16[48,1024]{1,0:T(8,128)(2,1)S(1)} %copy-done.2, bf16[48,1024]{1,0:T(8,128)(2,1)S(1)} %collective-permute-done.refs_1_, ...), custom_call_target="tpu_custom_call" | custom-call | tf_op jit(solution)/shard_map/attention/pallas_call | solution.py:163
  52.5 0.2 collective-permute-start.16
  52.7 1.4 %collective-permute-done.16 = bf16[128,1024]{1,0:T(8,128)(2,1)S(1)} collective-permute-done((bf16[128,1024]{1,0:T(8,128)(2,1)S(1)}, bf16[128,1024]{1,0:T(8,128)(2,1)S(1)}, u32[]{:S(2)}, u32[]{:S(2)}) %collective-permute-start.16) | collective-permute-done | bytes 262176 | tf_op jit(solution)/shard_map/ppermute | solution.py:192
  54.1 0.1 add_convert_fusion.1
  54.2 1.8 %collective-permute-start.17 = (bf16[128,1024]{1,0:T(8,128)(2,1)S(1)}, bf16[128,1024]{1,0:T(8,128)(2,1)S(1)}, u32[]{:S(2)}, u32[]{:S(2)}) collective-permute-start(bf16[128,1024]{1,0:T(8,128)(2,1)S(1)} %add_convert_fusion.1), channel_id=1, source_target_pairs={{0,1},{1,0},{2,3},{3,2},{4,5},{5,4},{6,7},{7,6},{8,9},{9,8},{10,11... | collective-permute-start | bytes 786440 | tf_op jit(solution)/shard_map/ppermute | solution.py:197
  56.0 6.7 %collective-permute-done.17 = bf16[128,1024]{1,0:T(8,128)(2,1)S(1)} collective-permute-done((bf16[128,1024]{1,0:T(8,128)(2,1)S(1)}, bf16[128,1024]{1,0:T(8,128)(2,1)S(1)}, u32[]{:S(2)}, u32[]{:S(2)}) %collective-permute-start.17) | collective-permute-done | bytes 262176 | tf_op jit(solution)/shard_map/ppermute | solution.py:197
  62.6 0.8 %add_convert_fusion = bf16[128,1024]{1,0:T(8,128)(2,1)} fusion(bf16[128,1024]{1,0:T(8,128)(2,1)S(1)} %collective-permute-done.17, bf16[128,1024]{1,0:T(8,128)(2,1)S(1)} %add_convert_fusion.1), kind=kLoop, calls=%fused_computation | loop fusion | flops 524288 | bytes 786432 | tf_op jit(solution)/shard_map/convert_element_type | solution.py:198
  (19 shorter events, 0.0 us)
Async XLA Ops:
  1.1 21.9 %collective-permute-start.15 = (bf16[128,2048]{1,0:T(8,128)(2,1)S(1)}, bf16[128,2048]{1,0:T(8,128)(2,1)S(1)}, u32[]{:S(2)}, u32[]{:S(2)}) collective-permute-start(bf16[128,2048]{1,0:T(8,128)(2,1)S(1)} %constant_dynamic-slice_fusion), channel_id=1, source_target_pairs={{0,2},{2,0},{4,6},{6,4},{8,10},{10,8},{12,14},{14,12},{16,18},{18,... | collective-permute-start | bytes 1572872 | tf_op jit(solution)/shard_map/ppermute | solution.py:158
  1.6 6.2 %collective-permute-start = (bf16[48,1024]{1,0:T(8,128)(2,1)}, bf16[48,1024]{1,0:T(8,128)(2,1)S(1)}, u32[]{:S(2)}, u32[]{:S(2)}) collective-permute-start(bf16[48,1024]{1,0:T(8,128)(2,1)} %refs_0_.1), channel_id=1, source_target_pairs={{0,8},{2,10},{4,0},{6,2},{8,16},{10,18},{12,4},{14,6},{16,24},{18,... | collective-permute-start | bytes 294920 | tf_op jit(solution)/shard_map/ppermute | solution.py:38
  4.2 5.4 %collective-permute-start.1 = (bf16[48,1024]{1,0:T(8,128)(2,1)}, bf16[48,1024]{1,0:T(8,128)(2,1)S(1)}, u32[]{:S(2)}, u32[]{:S(2)}) collective-permute-start(bf16[48,1024]{1,0:T(8,128)(2,1)} %refs_0_.1), channel_id=1, source_target_pairs={{0,4},{2,6},{4,12},{6,14},{8,0},{10,2},{12,20},{14,22},{16,8},{18,... | collective-permute-start | bytes 294920 | tf_op jit(solution)/shard_map/ppermute | solution.py:42
  7.8 4.6 %collective-permute-start.2 = (bf16[48,1024]{1,0:T(8,128)(2,1)S(1)}, bf16[48,1024]{1,0:T(8,128)(2,1)S(1)}, u32[]{:S(2)}, u32[]{:S(2)}) collective-permute-start(bf16[48,1024]{1,0:T(8,128)(2,1)S(1)} %collective-permute-done.refs_1_), channel_id=1, source_target_pairs={{0,8},{2,10},{4,0},{6,2},{8,16},{10,18},{12,4},{14,6},{16,24},{18,... | collective-permute-start | bytes 294920 | tf_op jit(solution)/shard_map/ppermute | solution.py:38
  9.6 4.6 %collective-permute-start.7 = (bf16[48,1024]{1,0:T(8,128)(2,1)}, bf16[48,1024]{1,0:T(8,128)(2,1)S(1)}, u32[]{:S(2)}, u32[]{:S(2)}) collective-permute-start(bf16[48,1024]{1,0:T(8,128)(2,1)} %refs_0_.1), channel_id=1, source_target_pairs={{0,2},{2,0},{4,6},{6,4},{8,10},{10,8},{12,14},{14,12},{16,18},{18,... | collective-permute-start | bytes 294920 | tf_op jit(solution)/shard_map/ppermute | solution.py:45
  9.6 5.2 %collective-permute-start.3 = (bf16[48,1024]{1,0:T(8,128)(2,1)S(1)}, bf16[48,1024]{1,0:T(8,128)(2,1)S(1)}, u32[]{:S(2)}, u32[]{:S(2)}) collective-permute-start(bf16[48,1024]{1,0:T(8,128)(2,1)S(1)} %collective-permute-done.1.refs_2_), channel_id=1, source_target_pairs={{0,4},{2,6},{4,12},{6,14},{8,0},{10,2},{12,20},{14,22},{16,8},{18,... | collective-permute-start | bytes 294920 | tf_op jit(solution)/shard_map/ppermute | solution.py:42
  9.8 5.3 %collective-permute-start.8 = (bf16[48,1024]{1,0:T(8,128)(2,1)S(1)}, bf16[48,1024]{1,0:T(8,128)(2,1)S(1)}, u32[]{:S(2)}, u32[]{:S(2)}) collective-permute-start(bf16[48,1024]{1,0:T(8,128)(2,1)S(1)} %collective-permute-done.refs_1_), channel_id=1, source_target_pairs={{0,2},{2,0},{4,6},{6,4},{8,10},{10,8},{12,14},{14,12},{16,18},{18,... | collective-permute-start | bytes 294920 | tf_op jit(solution)/shard_map/ppermute | solution.py:45
  12.4 4.6 %collective-permute-start.4 = (bf16[48,1024]{1,0:T(8,128)(2,1)S(1)}, bf16[48,1024]{1,0:T(8,128)(2,1)S(1)}, u32[]{:S(2)}, u32[]{:S(2)}) collective-permute-start(bf16[48,1024]{1,0:T(8,128)(2,1)S(1)} %collective-permute-done.2.refs_3_), channel_id=1, source_target_pairs={{0,8},{2,10},{4,0},{6,2},{8,16},{10,18},{12,4},{14,6},{16,24},{18,... | collective-permute-start | bytes 294920 | tf_op jit(solution)/shard_map/ppermute | solution.py:38
  14.2 4.6 %collective-permute-start.9 = (bf16[48,1024]{1,0:T(8,128)(2,1)S(1)}, bf16[48,1024]{1,0:T(8,128)(2,1)S(1)}, u32[]{:S(2)}, u32[]{:S(2)}) collective-permute-start(bf16[48,1024]{1,0:T(8,128)(2,1)S(1)} %collective-permute-done.1.refs_2_), channel_id=1, source_target_pairs={{0,2},{2,0},{4,6},{6,4},{8,10},{10,8},{12,14},{14,12},{16,18},{18,... | collective-permute-start | bytes 294920 | tf_op jit(solution)/shard_map/ppermute | solution.py:45
  14.8 4.6 %collective-permute-start.5 = (bf16[48,1024]{1,0:T(8,128)(2,1)S(1)}, bf16[48,1024]{1,0:T(8,128)(2,1)S(1)}, u32[]{:S(2)}, u32[]{:S(2)}) collective-permute-start(bf16[48,1024]{1,0:T(8,128)(2,1)S(1)} %collective-permute-done.3.refs_4_), channel_id=1, source_target_pairs={{0,4},{2,6},{4,12},{6,14},{8,0},{10,2},{12,20},{14,22},{16,8},{18,... | collective-permute-start | bytes 294920 | tf_op jit(solution)/shard_map/ppermute | solution.py:42
  15.1 4.3 %collective-permute-start.10 = (bf16[48,1024]{1,0:T(8,128)(2,1)S(1)}, bf16[48,1024]{1,0:T(8,128)(2,1)S(1)}, u32[]{:S(2)}, u32[]{:S(2)}) collective-permute-start(bf16[48,1024]{1,0:T(8,128)(2,1)S(1)} %collective-permute-done.2.refs_3_), channel_id=1, source_target_pairs={{0,2},{2,0},{4,6},{6,4},{8,10},{10,8},{12,14},{14,12},{16,18},{18,... | collective-permute-start | bytes 294920 | tf_op jit(solution)/shard_map/ppermute | solution.py:45
  17.0 4.6 %collective-permute-start.6 = (bf16[48,1024]{1,0:T(8,128)(2,1)S(1)}, bf16[48,1024]{1,0:T(8,128)(2,1)S(1)}, u32[]{:S(2)}, u32[]{:S(2)}) collective-permute-start(bf16[48,1024]{1,0:T(8,128)(2,1)S(1)} %collective-permute-done.4.refs_5_), channel_id=1, source_target_pairs={{0,8},{2,10},{4,0},{6,2},{8,16},{10,18},{12,4},{14,6},{16,24},{18,... | collective-permute-start | bytes 294920 | tf_op jit(solution)/shard_map/ppermute | solution.py:38
  18.8 3.5 %collective-permute-start.11 = (bf16[48,1024]{1,0:T(8,128)(2,1)S(1)}, bf16[48,1024]{1,0:T(8,128)(2,1)S(1)}, u32[]{:S(2)}, u32[]{:S(2)}) collective-permute-start(bf16[48,1024]{1,0:T(8,128)(2,1)S(1)} %collective-permute-done.3.refs_4_), channel_id=1, source_target_pairs={{0,2},{2,0},{4,6},{6,4},{8,10},{10,8},{12,14},{14,12},{16,18},{18,... | collective-permute-start | bytes 294920 | tf_op jit(solution)/shard_map/ppermute | solution.py:45
  19.4 2.9 %collective-permute-start.12 = (bf16[48,1024]{1,0:T(8,128)(2,1)S(1)}, bf16[48,1024]{1,0:T(8,128)(2,1)S(1)}, u32[]{:S(2)}, u32[]{:S(2)}) collective-permute-start(bf16[48,1024]{1,0:T(8,128)(2,1)S(1)} %collective-permute-done.4.refs_5_), channel_id=1, source_target_pairs={{0,2},{2,0},{4,6},{6,4},{8,10},{10,8},{12,14},{14,12},{16,18},{18,... | collective-permute-start | bytes 294920 | tf_op jit(solution)/shard_map/ppermute | solution.py:45
  19.4 2.9 %collective-permute-start.13 = (bf16[48,1024]{1,0:T(8,128)(2,1)S(1)}, bf16[48,1024]{1,0:T(8,128)(2,1)S(1)}, u32[]{:S(2)}, u32[]{:S(2)}) collective-permute-start(bf16[48,1024]{1,0:T(8,128)(2,1)S(1)} %collective-permute-done.5.refs_6_), channel_id=1, source_target_pairs={{0,2},{2,0},{4,6},{6,4},{8,10},{10,8},{12,14},{14,12},{16,18},{18,... | collective-permute-start | bytes 294920 | tf_op jit(solution)/shard_map/ppermute | solution.py:45
  21.6 1.3 %collective-permute-start.14 = (bf16[48,1024]{1,0:T(8,128)(2,1)S(1)}, bf16[48,1024]{1,0:T(8,128)(2,1)S(1)}, u32[]{:S(2)}, u32[]{:S(2)}) collective-permute-start(bf16[48,1024]{1,0:T(8,128)(2,1)S(1)} %collective-permute-done.6.refs_7_), channel_id=1, source_target_pairs={{0,2},{2,0},{4,6},{6,4},{8,10},{10,8},{12,14},{14,12},{16,18},{18,... | collective-permute-start | bytes 294920 | tf_op jit(solution)/shard_map/ppermute | solution.py:45
  22.9 3.4 %copy-start = (bf16[1024,4096]{1,0:T(8,128)(2,1)S(1)}, bf16[1024,4096]{1,0:T(8,128)(2,1)}, u32[]{:S(2)}) copy-start(bf16[1024,4096]{1,0:T(8,128)(2,1)} %refs_19_.1) | copy-start | bytes 25165828
  26.3 1.2 %copy-start.1 = (bf16[128,4096]{1,0:T(8,128)(2,1)S(1)}, bf16[128,4096]{1,0:T(8,128)(2,1)}, u32[]{:S(2)}) copy-start(bf16[128,4096]{1,0:T(8,128)(2,1)} %refs_17_.1) | copy-start | bytes 3145732
  27.6 0.9 %copy-start.2 = (bf16[48,1024]{1,0:T(8,128)(2,1)S(1)}, bf16[48,1024]{1,0:T(8,128)(2,1)}, u32[]{:S(2)}) copy-start(bf16[48,1024]{1,0:T(8,128)(2,1)} %refs_0_.1) | copy-start | bytes 294916
  28.4 0.7 %copy-start.3 = (s32[16,16]{1,0:T(8,128)S(1)}, s32[16,16]{1,0:T(8,128)}, u32[]{:S(2)}) copy-start(s32[16,16]{1,0:T(8,128)} %constant.27.clone.owners_ref) | copy-start | bytes 3076
  29.1 0.7 %copy-start.4 = (s32[3]{0:T(128)S(1)}, s32[3]{0:T(128)}, u32[]{:S(2)}) copy-start(s32[3]{0:T(128)} %length_ref.1) | copy-start | bytes 40
  52.5 1.6 %collective-permute-start.16 = (bf16[128,1024]{1,0:T(8,128)(2,1)S(1)}, bf16[128,1024]{1,0:T(8,128)(2,1)S(1)}, u32[]{:S(2)}, u32[]{:S(2)}) collective-permute-start(bf16[128,1024]{1,0:T(8,128)(2,1)S(1)} %get-tuple-element.8), channel_id=1, source_target_pairs={{0,2},{2,0},{4,6},{6,4},{8,10},{10,8},{12,14},{14,12},{16,18},{18,... | collective-permute-start | bytes 786440 | tf_op jit(solution)/shard_map/ppermute | solution.py:192
  54.2 8.4 %collective-permute-start.17 = (bf16[128,1024]{1,0:T(8,128)(2,1)S(1)}, bf16[128,1024]{1,0:T(8,128)(2,1)S(1)}, u32[]{:S(2)}, u32[]{:S(2)}) collective-permute-start(bf16[128,1024]{1,0:T(8,128)(2,1)S(1)} %add_convert_fusion.1), channel_id=1, source_target_pairs={{0,1},{1,0},{2,3},{3,2},{4,5},{5,4},{6,7},{7,6},{8,9},{9,8},{10,11... | collective-permute-start | bytes 786440 | tf_op jit(solution)/shard_map/ppermute | solution.py:197

commit v2 on v0

v2 whole, which is shorter than its diff:
```python
import functools

import jax
import jax.numpy as jnp
from jax import lax
from jax.experimental import pallas as pl
from jax.experimental.pallas import tpu as pltpu
from jax.sharding import PartitionSpec as P

DK = 128
PASS_LEN = 256
LOWEST = -1e30
TILE = 16
WIDE = 1024
HEADS_STEP = 8
ON_CHIP = pl.BlockSpec(memory_space=pltpu.VMEM)
SCALARS = pl.BlockSpec(memory_space=pltpu.SMEM)
FAR = pl.BlockSpec(memory_space=pltpu.HBM)


def params(mib):
    return pltpu.CompilerParams(vmem_limit_bytes=mib * 1024 * 1024)


def cost(flops, moved, exps=0):
    return pl.CostEstimate(flops=flops, bytes_accessed=moved, transcendentals=exps)


def chip_cycle(chips):
    up = list(range(0, chips, 2))
    return up + [chip for chip in range(chips - 1, -1, -1) if chip % 2]


def owner_of(device, source, chips):
    offset, crossed = source
    chip, core = device >> 1, device & 1
    place = jnp.where((chip & 1) == 0, chip >> 1, chips - ((chip + 1) >> 1)) + offset
    place = jnp.where(place < 0, place + chips, jnp.where(place >= chips, place - chips, place))
    chip = jnp.where(place < (chips + 1) >> 1, place << 1, ((chips - place) << 1) - 1)
    return (chip << 1) + (core ^ crossed)


class Plan:
    def __init__(self, order, rows_piece, passages):
        self.order, self.per_piece = order, rows_piece // TILE
        self.rows_piece, self.passages = rows_piece, passages
        self.tiles = len(order) * self.per_piece
        self.size = 2 * self.tiles + 2 + passages

    def write(self, plan, device, length_ref, chips):
        shift = PASS_LEN.bit_length() - 1
        for passage in range(self.passages):
            plan[2 * self.tiles + 2 + passage] = -1
        kept = jnp.int32(0)
        for index, source in enumerate(self.order):
            first = owner_of(device, source, chips) * self.rows_piece
            for tile in range(index * self.per_piece, (index + 1) * self.per_piece):
                row = first + (tile - index * self.per_piece) * TILE
                passage = row >> shift
                here = length_ref[passage] - (row & (PASS_LEN - 1))
                plan[tile] = here
                plan[self.tiles + tile] = kept

                @pl.when((here > 0) & (here < TILE))
                def _(kept=kept, here=here, passage=passage):
                    plan[2 * self.tiles + 2 + passage] = kept * TILE + here

                kept = kept + (here > 0).astype(jnp.int32)
        plan[2 * self.tiles] = kept
        plan[2 * self.tiles + 1] = device & 1

    def here(self, plan, tile):
        return plan[tile]

    def place(self, plan, tile):
        return plan[self.tiles + tile]

    def total(self, plan):
        return plan[2 * self.tiles]

    def core(self, plan):
        return plan[2 * self.tiles + 1]

    def partial(self, plan, passage):
        return plan[2 * self.tiles + 2 + passage]


def keep_valid(layout, plan, first, piece_refs, raw):
    begin = layout.place(plan, first * layout.per_piece)
    after = (first + len(piece_refs)) * layout.per_piece
    for index, piece_ref in enumerate(piece_refs):
        for tile in range(layout.per_piece):
            at = (first + index) * layout.per_piece + tile

            @pl.when(layout.here(plan, at) > 0)
            def _(at=at, tile=tile, piece_ref=piece_ref):
                row = pl.multiple_of((layout.place(plan, at) - begin) * TILE, TILE)
                raw[pl.ds(row, TILE), :] = piece_ref[tile * TILE:(tile + 1) * TILE, :]

    end = layout.place(plan, after) if after < layout.tiles else layout.total(plan)
    return begin, end - begin


def normalize(raw, rows, gain_ref, kept, number):
    wide = raw[:number, :].astype(jnp.float32)
    mean_square = jnp.mean(wide * wide, axis=-1, keepdims=True)
    scaled = wide * lax.rsqrt(mean_square + 1e-06) * gain_ref[...].astype(jnp.float32).reshape(1, -1)
    row = lax.broadcasted_iota(jnp.int32, scaled.shape, 0)
    rows[:number, :] = jnp.where(row < kept * TILE, scaled, 0.0).astype(jnp.bfloat16)


def stage_kernel(axis, device_ref, far, near, sem):
    half = near.shape[axis]
    ours = pl.ds(pl.multiple_of((device_ref[0] & 1) * half, half), half)
    copy = pltpu.make_async_copy(far.at[(slice(None),) * axis + (ours,)], near, sem)
    copy.start()
    copy.wait()


def stage(device, weight, axis):
    shape = tuple(size // 2 if at == axis else size for at, size in enumerate(weight.shape))
    return pl.pallas_call(
        functools.partial(stage_kernel, axis),
        in_specs=[SCALARS, FAR],
        out_specs=ON_CHIP,
        out_shape=jax.ShapeDtypeStruct(shape, weight.dtype),
        scratch_shapes=[pltpu.SemaphoreType.DMA],
        compiler_params=params(48),
        cost_estimate=cost(0, 2 * weight.size),
        name="stage",
    )(device, weight)


def begin_kernel(layout, chips, device_ref, length_far, gain_far, key_w_ref, value_far, queries_far, own_far,
                 crossed_ref, plan, gain_ref, value_w_ref, keys_ref, values_ref, own_q_ref, given_q_ref,
                 length_ref, own_ref, raw, rows, sems):
    device = device_ref[0]
    half = value_w_ref.shape[1]
    ours = pl.ds(pl.multiple_of((device & 1) * half, half), half)
    theirs = pl.ds(pl.multiple_of((1 - (device & 1)) * half, half), half)
    moves = (
        (length_far, length_ref),
        (own_far, own_ref),
        (gain_far, gain_ref),
        (value_far.at[:, ours], value_w_ref),
        (queries_far.at[:, ours], own_q_ref),
        (queries_far.at[:, theirs], given_q_ref),
    )
    copies = [
        pltpu.make_async_copy(source, target, sems.at[index])
        for index, (source, target) in enumerate(moves)
    ]
    for copy in copies:
        copy.start()
    copies[0].wait()
    layout.write(plan, device, length_ref, chips)
    copies[1].wait()
    _, kept = keep_valid(layout, plan, 0, [own_ref, crossed_ref], raw)
    copies[2].wait()
    number = raw.shape[0]
    normalize(raw, rows, gain_ref, kept, number)
    for weight_ref, out_ref in ((key_w_ref, keys_ref), (value_w_ref, values_ref)):
        if weight_ref is value_w_ref:
            for copy in copies[3:]:
                copy.wait()
        for left in range(0, half, WIDE):
            columns = slice(left, min(left + WIDE, half))
            out_ref[:number, columns] = jnp.dot(
                rows[...], weight_ref[:, columns], preferred_element_type=jnp.float32
            ).astype(jnp.bfloat16)


def begin(layout, chips, device, passage_length, gain, key_w, value_weight, queries, own, crossed, held_rows):
    width, half = key_w.shape
    held = jax.ShapeDtypeStruct((held_rows, half), jnp.bfloat16)
    query_half = jax.ShapeDtypeStruct((queries.shape[0], half), queries.dtype)
    return pl.pallas_call(
        functools.partial(begin_kernel, layout, chips),
        in_specs=[SCALARS, FAR, FAR, ON_CHIP, FAR, FAR, FAR, ON_CHIP],
        out_specs=[SCALARS] + [ON_CHIP] * 6,
        out_shape=[
            jax.ShapeDtypeStruct((layout.size,), jnp.int32),
            jax.ShapeDtypeStruct(gain.shape, gain.dtype),
            jax.ShapeDtypeStruct(key_w.shape, key_w.dtype),
            held, held, query_half, query_half,
        ],
        scratch_shapes=[
            pltpu.SMEM(passage_length.shape, jnp.int32),
            pltpu.VMEM(own.shape, own.dtype),
            pltpu.VMEM((2 * own.shape[0], width), jnp.bfloat16),
            pltpu.VMEM((2 * own.shape[0], width), jnp.bfloat16),
            pltpu.SemaphoreType.DMA((6,)),
        ],
        compiler_params=params(36),
        cost_estimate=cost(8 * own.shape[0] * width * half, 8 * width * half),
        name="begin",
    )(device, passage_length, gain, key_w, value_weight, queries, own, crossed)


def project_kernel(layout, first, count, cases, stages, plan, gain_ref, key_w_ref, value_w_ref, *refs):
    piece_refs = refs[:count]
    if stages:
        out_far, out_w_ref, sem = refs[count], refs[-4], refs[-1]
        refs = refs[:-4] + refs[-3:-1]
        half = out_w_ref.shape[0]
        ours = pl.ds(pl.multiple_of(layout.core(plan) * half, half), half)
        staging = pltpu.make_async_copy(out_far.at[ours, :], out_w_ref, sem)
        staging.start()
    keys_ref, values_ref, raw, rows = refs[-4:]
    begin_tile, kept = keep_valid(layout, plan, first, piece_refs, raw)
    start = pl.multiple_of(begin_tile * TILE, TILE)
    width = key_w_ref.shape[1]

    def project(number):
        normalize(raw, rows, gain_ref, kept, number)
        for left in range(0, width, WIDE):
            columns = slice(left, min(left + WIDE, width))
            for weight_ref, out_ref in ((key_w_ref, keys_ref), (value_w_ref, values_ref)):
                out_ref[pl.ds(start, number), columns] = jnp.dot(
                    rows[:number, :], weight_ref[:, columns], preferred_element_type=jnp.float32
                ).astype(jnp.bfloat16)

    low = 0
    for number in cases:
        pl.when((kept * TILE > low) & (kept * TILE <= number))(functools.partial(project, number))
        low = number
    if stages:
        staging.wait()


def project(layout, first, plan, gain, key_w, value_w, pieces, held, out_weight=None):
    rows_now = len(pieces) * layout.rows_piece
    width, half = key_w.shape
    cases = sorted({-(-rows_now * part // 3 // TILE) * TILE for part in (2, 3)})
    stages = out_weight is not None
    shapes = [jax.ShapeDtypeStruct(held[0].shape, jnp.bfloat16)] * 2
    if stages:
        shapes.append(jax.ShapeDtypeStruct((half, out_weight.shape[1]), out_weight.dtype))
    at = 4 + len(pieces) + stages
    return pl.pallas_call(
        functools.partial(project_kernel, layout, first, len(pieces), cases, stages),
        in_specs=[SCALARS] + [ON_CHIP] * (3 + len(pieces)) + [FAR] * stages + [ON_CHIP] * 2,
        out_specs=[ON_CHIP] * len(shapes),
        out_shape=shapes,
        scratch_shapes=[pltpu.VMEM((rows_now, width), jnp.bfloat16)] * 2 + [pltpu.SemaphoreType.DMA] * stages,
        input_output_aliases={at: 0, at + 1: 1},
        compiler_params=params(28 if stages else 16),
        cost_estimate=cost(4 * rows_now * width * half, 4 * width * half),
        name="project",
    )(plan, gain, key_w, value_w, *pieces, *([out_weight] if stages else []), *held)


def attend_kernel(layout, cases, plan, own_q_ref, other_q_ref, keys_ref, values_ref, out_w_ref,
                  own_ref, other_ref, bias, total):
    half, inner = own_q_ref.shape
    kept = layout.total(plan)
    lane = lax.broadcasted_iota(jnp.int32, bias.shape, 1)
    valid = lane < kept * TILE
    for passage in range(layout.passages):
        begin = layout.partial(plan, passage)
        end = ((begin + TILE - 1) >> (TILE.bit_length() - 1)) * TILE
        valid = valid & ((begin < 0) | (lane < begin) | (lane >= end))
    bias[...] = jnp.where(valid, 0.0, LOWEST)

    def attend_heads(number, count, left):
        columns = pl.ds(left, count * DK)
        query_rows = jnp.concatenate([own_q_ref[:, columns], other_q_ref[:, columns]], axis=0)
        key_rows, value_rows = keys_ref[:number, columns], values_ref[:number, columns]
        attended = []
        for head in range(count):
            here = slice(head * DK, (head + 1) * DK)
            scores = lax.dot_general(
                query_rows[:, here], key_rows[:, here],
                (((1,), (1,)), ((), ())), preferred_element_type=jnp.float32,
            ) + bias[0:1, :number]
            top = jnp.max(scores, axis=-1, keepdims=True)
            expo = jnp.exp(scores - top)
            denom = jnp.sum(expo, axis=-1, keepdims=True)
            mixed = jnp.dot(
                expo.astype(jnp.bfloat16), value_rows[:, here], preferred_element_type=jnp.float32
            )
            attended.append((mixed / denom).astype(jnp.bfloat16))
        return jnp.concatenate(attended, axis=1)

    def attend(number, count):
        def clear(tile, carry):
            at = pl.ds(pl.multiple_of(tile * TILE, TILE), TILE)
            keys_ref[at, :] = jnp.zeros((TILE, inner), jnp.bfloat16)
            values_ref[at, :] = jnp.zeros((TILE, inner), jnp.bfloat16)
            return carry

        lax.fori_loop(kept, number // TILE, clear, 0)

        def heads(step, carry):
            left = pl.multiple_of(step * count * DK, count * DK)
            attended = attend_heads(number, count, left)
            product = jnp.dot(attended, out_w_ref[pl.ds(left, count * DK), :], preferred_element_type=jnp.float32)

            @pl.when(step == 0)
            def _():
                total[...] = product

            @pl.when(step > 0)
            def _():
                total[...] += product

            return carry

        lax.fori_loop(0, inner // (count * DK), heads, 0)

    low = 0
    for number in cases:
        count = 1 if number == cases[-1] else HEADS_STEP
        pl.when((kept * TILE > low) & (kept * TILE <= number))(functools.partial(attend, number, count))
        low = number
    own_ref[...] = total[:half, :].astype(jnp.bfloat16)
    other_ref[...] = total[half:, :].astype(jnp.bfloat16)


def attend(layout, plan, own_q, other_q, keys, values, out_w):
    rows_here, half = own_q.shape
    width = out_w.shape[1]
    enc_rows = layout.tiles * TILE
    cases = [enc_rows * part // 12 // 64 * 64 for part in (8, 9)] + [enc_rows]
    return pl.pallas_call(
        functools.partial(attend_kernel, layout, cases),
        in_specs=[SCALARS] + [ON_CHIP] * 5,
        out_specs=[ON_CHIP] * 2,
        out_shape=[jax.ShapeDtypeStruct((rows_here, width), jnp.bfloat16)] * 2,
        scratch_shapes=[
            pltpu.VMEM((8, enc_rows), jnp.float32),
            pltpu.VMEM((2 * rows_here, width), jnp.float32),
        ],
        compiler_params=params(24),
        cost_estimate=cost(4 * rows_here * (2 * enc_rows + width) * half, 2 * half * width),
        name="attend",
    )(plan, own_q, other_q, keys, values, out_w)


def on_device(number, queries, passages, enc_gain, key_weight, value_weight, out_weight, passage_length):
    rows_piece = passages.shape[0]
    heads_axis = lax.axis_size("heads")
    chips = number // 2
    cycle = chip_cycle(chips)
    place = {chip: index for index, chip in enumerate(cycle)}
    other_core = [(device, device ^ 1) for device in range(number)]

    def hop(by, crossed=0):
        return [
            (2 * chip + core, 2 * cycle[(place[chip] + by) % chips] + (core ^ crossed))
            for chip in range(chips)
            for core in range(2)
        ]

    def cross(piece):
        return lax.ppermute(piece, "rows", other_core)

    rounds = []
    for step in range(1, chips // 2 + 1):
        if 2 * step == chips:
            rounds.append([(-step, 0), (step, 1)])
        else:
            rounds.append([(-step, 0), (step, 0), (-step, 1), (step, 1)])
    order = [(0, 0), (0, 1)] + [source for sources in rounds for source in sources]
    layout = Plan(order, rows_piece, passage_length.shape[0])

    device = lax.axis_index("rows").reshape(1)
    held_rows = number * rows_piece + 4 * rows_piece
    key_w = stage(device, key_weight, 1)
    plan, gain, value_w, *held, own_q, given_q = begin(
        layout, chips, device, passage_length, enc_gain, key_w, value_weight,
        queries, passages, cross(passages), held_rows,
    )
    other_q = cross(given_q)

    ahead = lax.ppermute(passages, "rows", hop(1))
    behind = lax.ppermute(passages, "rows", hop(-1, len(rounds[0]) == 2))
    first, out_w = 2, None
    staged_by = max(0, len(rounds) - 2)
    for index, (sources, later) in enumerate(zip(rounds, rounds[1:] + [None])):
        ahead, behind, *held = lax.optimization_barrier((ahead, behind, *held))
        pieces = [ahead, behind]
        if len(sources) > 2:
            pieces += [cross(ahead), cross(behind)]
        if later:
            ahead = lax.ppermute(ahead, "rows", hop(1))
            behind = lax.ppermute(behind, "rows", hop(-1, len(later) == 2))
        *held, last = project(
            layout, first, plan, gain, key_w, value_w, pieces, held, out_weight if index == staged_by else None
        )
        if index == staged_by:
            out_w = last
        else:
            held.append(last)
        first += len(pieces)
    keys, values = held

    own, other = attend(layout, plan, own_q, other_q, keys, values, out_w)
    share = (own.astype(jnp.float32) + cross(other).astype(jnp.float32)).astype(jnp.bfloat16)
    by = 1
    while by < heads_axis:
        turn = [(place, place ^ by) for place in range(heads_axis)]
        given = lax.ppermute(share, "heads", turn)
        share = (share.astype(jnp.float32) + given.astype(jnp.float32)).astype(jnp.bfloat16)
        by *= 2
    return share


def solution(mesh):
    return jax.shard_map(
        functools.partial(on_device, mesh.shape["rows"]),
        mesh=mesh,
        in_specs=(
            P(("groups", "rows"), "heads"),
            P(("groups", "rows"), None),
            P(),
            P(None, "heads"),
            P(None, "heads"),
            P("heads", None),
            P("groups"),
        ),
        out_specs=P(("groups", "rows"), None),
        check_vma=False,
    )
```

time: 133 us -> 49.3 us (0.37)
  waiting for transfers between devices: 54.7 us -> 14.3 us
  matrix products: 40 us -> 0 us
  Pallas kernels: 0 us -> 21.5 us
  between operations: 13.5 us -> 0.13 us
  local copies, waits for them, and re-layouts: 12.3 us -> 0.17 us
  starting transfers between devices: 0.04 us -> 12 us
  blocking collectives: 6.12 us -> 0 us
  other arithmetic: 6.14 us -> 0.84 us
    all_gather x1 -> x0, waiting for transfers between devices: 43.3 us -> none  [on_device(): lax.all_gather(passages, 'rows', axis=0, tiled=True)]
    dot_general x5 -> x0, matrix products: 40 us -> none  [the longest x1 12.5 us: project(): jnp.dot(normed, value_weight, preferred_element_type=jnp.float32)]
    pallas_call x0 -> x7, Pallas kernels: none -> 21.5 us  [the longest x4 8.84 us: project(): pl.pallas_call(functools.partial(project_kernel, layout, first, len(piece...]
    ppermute x0 -> x18, waiting for transfers between devices: none -> 14.3 us  [the longest x1 6.83 us: on_device(): given = lax.ppermute(share, 'heads', turn)]
    ppermute x0 -> x18, starting transfers between devices: none -> 12 us  [the longest x3 5.17 us: on_device(): ahead = lax.ppermute(ahead, 'rows', hop(1))]
    reduce_scatter x1 -> x0, waiting for transfers between devices: 10.7 us -> none  [on_device(): lax.psum_scatter(partial_out.astype(jnp.bfloat16), 'heads', scatter_dimen...]
    reshape x1 -> x0, local copies, waits for them, and re-layouts: 8.82 us -> none  [attend(): value_heads = value_rows.reshape(number, heads_here, DK)]
    all_gather x1 -> x0, blocking collectives: 6.12 us -> none  [on_device(): cross_out = lax.all_gather(share, 'heads', axis=1, tiled=True)]
  transfers between devices with their start and end apart: 2 -> 18, of which waited for: 2 -> 8; matrix products, arithmetic and copies ran while one was open for 1% -> 0% of each run, Pallas kernels for 0% -> 29%
where the time goes in v2:
time: 49.3 us; the launch traced here: 48.9 us
  Pallas kernels  21.5 us (44%)
  waiting for transfers between devices  14.3 us (29%)
  starting transfers between devices  12 us (24%)
  other arithmetic  0.84 us (2%)
    pallas_call x4, Pallas kernels, project(): pl.pallas_call(functools.partial(project_kernel, layout, first, len(piece...  8.84 us
    pallas_call x1, Pallas kernels, attend(): pl.pallas_call(functools.partial(attend_kernel, layout, cases), in_specs=...  7.18 us
    ppermute x1, waiting for transfers between devices, on_device(): given = lax.ppermute(share, 'heads', turn)  6.83 us
    ppermute x3, starting transfers between devices, on_device(): ahead = lax.ppermute(ahead, 'rows', hop(1))  5.17 us
    ppermute x3, waiting for transfers between devices, on_device(): behind = lax.ppermute(behind, 'rows', hop(-1, len(later) == 2))  4.82 us
    pallas_call x1, Pallas kernels, begin(): pl.pallas_call(functools.partial(begin_kernel, layout, chips), in_specs=[...  3.2 us
    ppermute x1, starting transfers between devices, on_device(): ahead = lax.ppermute(passages, 'rows', hop(1))  2.57 us
    pallas_call x1, Pallas kernels, stage(): pl.pallas_call(functools.partial(stage_kernel, axis), in_specs=[SCALARS,...  2.29 us
  transfers between devices with their start and end apart: 18, of which 8 were waited for; matrix products, arithmetic and copies ran while one was open for 0% of the time, Pallas kernels for 29%

profile of v2, /device:TPU:0, one launch (start us, length us, event | category | flops | bytes accessed | tf_op | source)
XLA Modules:
  0.0 48.9 jit_solution(6727448132264559559)
XLA Ops:
  0.0 0.5 collective-permute-start
  0.5 2.6 %collective-permute-start.2 = (bf16[48,1024]{1,0:T(8,128)(2,1)}, bf16[48,1024]{1,0:T(8,128)(2,1)S(1)}, u32[]{:S(2)}, u32[]{:S(2)}) collective-permute-start(bf16[48,1024]{1,0:T(8,128)(2,1)} %own_far.1), channel_id=1, source_target_pairs={{0,8},{2,10},{4,0},{6,2},{8,16},{10,18},{12,4},{14,6},{16,24},{18,... | collective-permute-start | bytes 294920 | tf_op jit(solution)/shard_map/ppermute | solution.py:376
  3.0 0.0 collective-permute-start.3
  3.1 2.3 %stage.1.key_w_ref = bf16[1024,2048]{1,0:T(8,128)(2,1)S(1)} custom-call(s32[1]{0:T(128)} %bitcast.device_ref, bf16[1024,4096]{1,0:T(8,128)(2,1)} %far.1), custom_call_target="tpu_custom_call" | custom-call | bytes 8388608 | tf_op jit(solution)/shard_map/stage/pallas_call | solution.py:122
  5.4 0.2 copy-done
  5.5 3.2 %begin.1 = (s32[101]{0:T(128)S(1)}, bf16[1024]{0:T(1024)(128)(2,1)S(1)}, bf16[1024,2048]{1,0:T(8,128)(2,1)S(1)}, bf16[960,2048]{1,0:T(8,128)(2,1)S(1)}, bf16[960...) custom-call(s32[1]{0:T(128)} %bitcast.device_ref, s32[3]{0:T(128)S(1)} %copy-done.3, ...), custom_call_target="tpu_custom_call" | custom-call | flops 805306368 | bytes 16777216 | tf_op jit(solution)/shard_map/begin/pallas_call | solution.py:177
  8.8 0.3 collective-permute-start.6
  9.0 0.3 collective-permute-start.7
  9.3 2.0 %collective-permute-start.4 = (bf16[48,1024]{1,0:T(8,128)(2,1)S(1)}, bf16[48,1024]{1,0:T(8,128)(2,1)S(1)}, u32[]{:S(2)}, u32[]{:S(2)}) collective-permute-start(bf16[48,1024]{1,0:T(8,128)(2,1)S(1)} %collective-permute-done.2.refs_0_), channel_id=1, source_target_pairs={{0,8},{2,10},{4,0},{6,2},{8,16},{10,18},{12,4},{14,6},{16,24},{18,... | collective-permute-start | bytes 294920 | tf_op jit(solution)/shard_map/ppermute | solution.py:386
  11.4 2.7 %project.4 = (bf16[960,2048]{1,0:T(8,128)(2,1)S(1)}, bf16[960,2048]{1,0:T(8,128)(2,1)S(1)}) custom-call(s32[101]{0:T(128)S(1)} %get-tuple-element.39.plan, bf16[1024]{0:T(1024)(128)(2,1)S(1)} %get-tuple-element.42.gain_ref, bf16[1024,2048]{1,0:T(8,128)(2,1)S(1)} %stage.1.key_w_ref, ...), custom_call_target="tpu_custom_call", output_to_operand_aliasing={{0}: (8, {}), {1}: (9, {})} | custom-call | flops 1610612736 | bytes 8388608 | tf_op jit(solution)/shard_map/project/pallas_call | solution.py:240
  14.0 0.3 collective-permute-done.4.refs_0_
  14.3 1.6 %collective-permute-done.5.refs_1_ = bf16[48,1024]{1,0:T(8,128)(2,1)S(1)} collective-permute-done((bf16[48,1024]{1,0:T(8,128)(2,1)S(1)}, bf16[48,1024]{1,0:T(8,128)(2,1)S(1)}, u32[]{:S(2)}, u32[]{:S(2)}) %collective-permute-start.5) | collective-permute-done | bytes 98336 | tf_op jit(solution)/shard_map/ppermute | solution.py:387
  16.0 0.5 %collective-permute-start.11 = (bf16[48,1024]{1,0:T(8,128)(2,1)S(1)}, bf16[48,1024]{1,0:T(8,128)(2,1)S(1)}, u32[]{:S(2)}, u32[]{:S(2)}) collective-permute-start(bf16[48,1024]{1,0:T(8,128)(2,1)S(1)} %collective-permute-done.5.refs_1_), channel_id=1, source_target_pairs={{0,2},{2,0},{4,6},{6,4},{8,10},{10,8},{12,14},{14,12},{16,18},{18,... | collective-permute-start | bytes 294920 | tf_op jit(solution)/shard_map/ppermute | solution.py:356
  16.5 0.0 collective-permute-start.1
  16.5 1.6 %collective-permute-start.8 = (bf16[48,1024]{1,0:T(8,128)(2,1)S(1)}, bf16[48,1024]{1,0:T(8,128)(2,1)S(1)}, u32[]{:S(2)}, u32[]{:S(2)}) collective-permute-start(bf16[48,1024]{1,0:T(8,128)(2,1)S(1)} %collective-permute-done.4.refs_0_), channel_id=1, source_target_pairs={{0,8},{2,10},{4,0},{6,2},{8,16},{10,18},{12,4},{14,6},{16,24},{18,... | collective-permute-start | bytes 294920 | tf_op jit(solution)/shard_map/ppermute | solution.py:386
  18.1 0.5 collective-permute-start.9
  18.5 2.6 %project.5 = (bf16[960,2048]{1,0:T(8,128)(2,1)S(1)}, bf16[960,2048]{1,0:T(8,128)(2,1)S(1)}) custom-call(s32[101]{0:T(128)S(1)} %get-tuple-element.39.plan, bf16[1024]{0:T(1024)(128)(2,1)S(1)} %get-tuple-element.42.gain_ref, bf16[1024,2048]{1,0:T(8,128)(2,1)S(1)} %stage.1.key_w_ref, ...), custom_call_target="tpu_custom_call", output_to_operand_aliasing={{0}: (8, {}), {1}: (9, {})} | custom-call | flops 1610612736 | bytes 8388608 | tf_op jit(solution)/shard_map/project/pallas_call | solution.py:240
  21.2 0.5 %collective-permute-done.8.refs_0_ = bf16[48,1024]{1,0:T(8,128)(2,1)S(1)} collective-permute-done((bf16[48,1024]{1,0:T(8,128)(2,1)S(1)}, bf16[48,1024]{1,0:T(8,128)(2,1)S(1)}, u32[]{:S(2)}, u32[]{:S(2)}) %collective-permute-start.8) | collective-permute-done | bytes 98336 | tf_op jit(solution)/shard_map/ppermute | solution.py:386
  21.7 1.3 %collective-permute-done.9.refs_1_ = bf16[48,1024]{1,0:T(8,128)(2,1)S(1)} collective-permute-done((bf16[48,1024]{1,0:T(8,128)(2,1)S(1)}, bf16[48,1024]{1,0:T(8,128)(2,1)S(1)}, u32[]{:S(2)}, u32[]{:S(2)}) %collective-permute-start.9) | collective-permute-done | bytes 98336 | tf_op jit(solution)/shard_map/ppermute | solution.py:387
  23.0 0.5 %collective-permute-start.15 = (bf16[48,1024]{1,0:T(8,128)(2,1)S(1)}, bf16[48,1024]{1,0:T(8,128)(2,1)S(1)}, u32[]{:S(2)}, u32[]{:S(2)}) collective-permute-start(bf16[48,1024]{1,0:T(8,128)(2,1)S(1)} %collective-permute-done.9.refs_1_), channel_id=1, source_target_pairs={{0,2},{2,0},{4,6},{6,4},{8,10},{10,8},{12,14},{14,12},{16,18},{18,... | collective-permute-start | bytes 294920 | tf_op jit(solution)/shard_map/ppermute | solution.py:356
  23.5 1.6 %collective-permute-start.12 = (bf16[48,1024]{1,0:T(8,128)(2,1)S(1)}, bf16[48,1024]{1,0:T(8,128)(2,1)S(1)}, u32[]{:S(2)}, u32[]{:S(2)}) collective-permute-start(bf16[48,1024]{1,0:T(8,128)(2,1)S(1)} %collective-permute-done.8.refs_0_), channel_id=1, source_target_pairs={{0,8},{2,10},{4,0},{6,2},{8,16},{10,18},{12,4},{14,6},{16,24},{18,... | collective-permute-start | bytes 294920 | tf_op jit(solution)/shard_map/ppermute | solution.py:386
  25.1 2.7 %project.6 = (bf16[960,2048]{1,0:T(8,128)(2,1)S(1)}, bf16[960,2048]{1,0:T(8,128)(2,1)S(1)}, bf16[2048,1024]{1,0:T(8,128)(2,1)S(1)}) custom-call(s32[101]{0:T(128)S(1)} %get-tuple-element.39.plan, bf16[1024]{0:T(1024)(128)(2,1)S(1)} %get-tuple-element.42.gain_ref, ...), custom_call_target="tpu_custom_call", output_to_operand_aliasing={{0}: (9, {}), {1}: (10, {})} | custom-call | flops 1610612736 | bytes 8388608 | tf_op jit(solution)/shard_map/project/pallas_call | solution.py:240
  27.8 0.4 collective-permute-done.12.refs_0_
  28.2 1.9 %collective-permute-done.13.refs_1_ = bf16[48,1024]{1,0:T(8,128)(2,1)S(1)} collective-permute-done((bf16[48,1024]{1,0:T(8,128)(2,1)S(1)}, bf16[48,1024]{1,0:T(8,128)(2,1)S(1)}, u32[]{:S(2)}, u32[]{:S(2)}) %collective-permute-start.13) | collective-permute-done | bytes 98336 | tf_op jit(solution)/shard_map/ppermute | solution.py:387
  30.1 0.8 %project.7 = (bf16[960,2048]{1,0:T(8,128)(2,1)S(1)}, bf16[960,2048]{1,0:T(8,128)(2,1)S(1)}) custom-call(s32[101]{0:T(128)S(1)} %get-tuple-element.39.plan, bf16[1024]{0:T(1024)(128)(2,1)S(1)} %get-tuple-element.42.gain_ref, bf16[1024,2048]{1,0:T(8,128)(2,1)S(1)} %stage.1.key_w_ref, ...), custom_call_target="tpu_custom_call", output_to_operand_aliasing={{0}: (6, {}), {1}: (7, {})} | custom-call | flops 805306368 | bytes 8388608 | tf_op jit(solution)/shard_map/project/pallas_call | solution.py:240
  30.9 7.2 %attend.1 = (bf16[128,1024]{1,0:T(8,128)(2,1)S(1)}, bf16[128,1024]{1,0:T(8,128)(2,1)S(1)}) custom-call(s32[101]{0:T(128)S(1)} %get-tuple-element.39.plan, bf16[128,2048]{1,0:T(8,128)(2,1)S(1)} %get-tuple-element.40.own_q_ref, bf16[128,2048]{1,0:T(8,128)(2,1)S(1)} %collective-permute-done.1.other_q_ref, bf16[960,2048]{1,0:T(8,128)(2,1)S(1)} %get-tuple-element.68.keys_ref, ...), custom_call_target="tpu_custom_call" | custom-call | flops 2684354560 | bytes 4194304 | tf_op jit(solution)/shard_map/attend/pallas_call | solution.py:325
  38.1 0.2 collective-permute-start.16
  38.3 1.4 %collective-permute-done.16 = bf16[128,1024]{1,0:T(8,128)(2,1)S(1)} collective-permute-done((bf16[128,1024]{1,0:T(8,128)(2,1)S(1)}, bf16[128,1024]{1,0:T(8,128)(2,1)S(1)}, u32[]{:S(2)}, u32[]{:S(2)}) %collective-permute-start.16) | collective-permute-done | bytes 262176 | tf_op jit(solution)/shard_map/ppermute | solution.py:356
  39.7 0.1 add_convert_fusion.1
  39.7 1.6 %collective-permute-start.17 = (bf16[128,1024]{1,0:T(8,128)(2,1)S(1)}, bf16[128,1024]{1,0:T(8,128)(2,1)S(1)}, u32[]{:S(2)}, u32[]{:S(2)}) collective-permute-start(bf16[128,1024]{1,0:T(8,128)(2,1)S(1)} %add_convert_fusion.1), channel_id=1, source_target_pairs={{0,1},{1,0},{2,3},{3,2},{4,5},{5,4},{6,7},{7,6},{8,9},{9,8},{10,11... | collective-permute-start | bytes 786440 | tf_op jit(solution)/shard_map/ppermute | solution.py:403
  41.3 6.8 %collective-permute-done.17 = bf16[128,1024]{1,0:T(8,128)(2,1)S(1)} collective-permute-done((bf16[128,1024]{1,0:T(8,128)(2,1)S(1)}, bf16[128,1024]{1,0:T(8,128)(2,1)S(1)}, u32[]{:S(2)}, u32[]{:S(2)}) %collective-permute-start.17) | collective-permute-done | bytes 262176 | tf_op jit(solution)/shard_map/ppermute | solution.py:403
  48.2 0.8 %add_convert_fusion = bf16[128,1024]{1,0:T(8,128)(2,1)} fusion(bf16[128,1024]{1,0:T(8,128)(2,1)S(1)} %collective-permute-done.17, bf16[128,1024]{1,0:T(8,128)(2,1)S(1)} %add_convert_fusion.1), kind=kLoop, calls=%fused_computation | loop fusion | flops 524288 | bytes 786432 | tf_op jit(solution)/shard_map/convert_element_type | solution.py:404
  (21 shorter events, 0.0 us)
Async XLA Ops:
  0.0 5.4 %collective-permute-start = (bf16[48,1024]{1,0:T(8,128)(2,1)}, bf16[48,1024]{1,0:T(8,128)(2,1)S(1)}, u32[]{:S(2)}, u32[]{:S(2)}) collective-permute-start(bf16[48,1024]{1,0:T(8,128)(2,1)} %own_far.1), channel_id=1, source_target_pairs={{0,2},{2,0},{4,6},{6,4},{8,10},{10,8},{12,14},{14,12},{16,18},{18,... | collective-permute-start | bytes 294920 | tf_op jit(solution)/shard_map/ppermute | solution.py:356
  0.5 8.3 %collective-permute-start.2 = (bf16[48,1024]{1,0:T(8,128)(2,1)}, bf16[48,1024]{1,0:T(8,128)(2,1)S(1)}, u32[]{:S(2)}, u32[]{:S(2)}) collective-permute-start(bf16[48,1024]{1,0:T(8,128)(2,1)} %own_far.1), channel_id=1, source_target_pairs={{0,8},{2,10},{4,0},{6,2},{8,16},{10,18},{12,4},{14,6},{16,24},{18,... | collective-permute-start | bytes 294920 | tf_op jit(solution)/shard_map/ppermute | solution.py:376
  3.0 5.7 %collective-permute-start.3 = (bf16[48,1024]{1,0:T(8,128)(2,1)}, bf16[48,1024]{1,0:T(8,128)(2,1)S(1)}, u32[]{:S(2)}, u32[]{:S(2)}) collective-permute-start(bf16[48,1024]{1,0:T(8,128)(2,1)} %own_far.1), channel_id=1, source_target_pairs={{0,4},{2,6},{4,12},{6,14},{8,0},{10,2},{12,20},{14,22},{16,8},{18,... | collective-permute-start | bytes 294920 | tf_op jit(solution)/shard_map/ppermute | solution.py:377
  3.0 2.5 %copy-start = (bf16[128,4096]{1,0:T(8,128)(2,1)S(1)}, bf16[128,4096]{1,0:T(8,128)(2,1)}, u32[]{:S(2)}) copy-start(bf16[128,4096]{1,0:T(8,128)(2,1)} %queries_far.1) | copy-start | bytes 3145732
  3.0 2.5 %copy-start.1 = (bf16[48,1024]{1,0:T(8,128)(2,1)S(1)}, bf16[48,1024]{1,0:T(8,128)(2,1)}, u32[]{:S(2)}) copy-start(bf16[48,1024]{1,0:T(8,128)(2,1)} %own_far.1) | copy-start | bytes 294916
  3.0 2.5 %copy-start.2 = (bf16[1024]{0:T(1024)(128)(2,1)S(1)}, bf16[1024]{0:T(1024)(128)(2,1)}, u32[]{:S(2)}) copy-start(bf16[1024]{0:T(1024)(128)(2,1)} %gain_far.1) | copy-start | bytes 6148
  3.0 2.5 %copy-start.3 = (s32[3]{0:T(128)S(1)}, s32[3]{0:T(128)}, u32[]{:S(2)}) copy-start(s32[3]{0:T(128)} %length_far.1) | copy-start | bytes 40
  8.8 2.6 %collective-permute-start.6 = (bf16[48,1024]{1,0:T(8,128)(2,1)S(1)}, bf16[48,1024]{1,0:T(8,128)(2,1)S(1)}, u32[]{:S(2)}, u32[]{:S(2)}) collective-permute-start(bf16[48,1024]{1,0:T(8,128)(2,1)S(1)} %collective-permute-done.2.refs_0_), channel_id=1, source_target_pairs={{0,2},{2,0},{4,6},{6,4},{8,10},{10,8},{12,14},{14,12},{16,18},{18,... | collective-permute-start | bytes 294920 | tf_op jit(solution)/shard_map/ppermute | solution.py:356
  9.0 2.3 %collective-permute-start.7 = (bf16[48,1024]{1,0:T(8,128)(2,1)S(1)}, bf16[48,1024]{1,0:T(8,128)(2,1)S(1)}, u32[]{:S(2)}, u32[]{:S(2)}) collective-permute-start(bf16[48,1024]{1,0:T(8,128)(2,1)S(1)} %collective-permute-done.3.refs_1_), channel_id=1, source_target_pairs={{0,2},{2,0},{4,6},{6,4},{8,10},{10,8},{12,14},{14,12},{16,18},{18,... | collective-permute-start | bytes 294920 | tf_op jit(solution)/shard_map/ppermute | solution.py:356
  9.3 5.0 %collective-permute-start.4 = (bf16[48,1024]{1,0:T(8,128)(2,1)S(1)}, bf16[48,1024]{1,0:T(8,128)(2,1)S(1)}, u32[]{:S(2)}, u32[]{:S(2)}) collective-permute-start(bf16[48,1024]{1,0:T(8,128)(2,1)S(1)} %collective-permute-done.2.refs_0_), channel_id=1, source_target_pairs={{0,8},{2,10},{4,0},{6,2},{8,16},{10,18},{12,4},{14,6},{16,24},{18,... | collective-permute-start | bytes 294920 | tf_op jit(solution)/shard_map/ppermute | solution.py:386
  11.4 4.6 %collective-permute-start.5 = (bf16[48,1024]{1,0:T(8,128)(2,1)S(1)}, bf16[48,1024]{1,0:T(8,128)(2,1)S(1)}, u32[]{:S(2)}, u32[]{:S(2)}) collective-permute-start(bf16[48,1024]{1,0:T(8,128)(2,1)S(1)} %collective-permute-done.3.refs_1_), channel_id=1, source_target_pairs={{0,4},{2,6},{4,12},{6,14},{8,0},{10,2},{12,20},{14,22},{16,8},{18,... | collective-permute-start | bytes 294920 | tf_op jit(solution)/shard_map/ppermute | solution.py:387
  16.0 2.5 %collective-permute-start.10 = (bf16[48,1024]{1,0:T(8,128)(2,1)S(1)}, bf16[48,1024]{1,0:T(8,128)(2,1)S(1)}, u32[]{:S(2)}, u32[]{:S(2)}) collective-permute-start(bf16[48,1024]{1,0:T(8,128)(2,1)S(1)} %collective-permute-done.4.refs_0_), channel_id=1, source_target_pairs={{0,2},{2,0},{4,6},{6,4},{8,10},{10,8},{12,14},{14,12},{16,18},{18,... | collective-permute-start | bytes 294920 | tf_op jit(solution)/shard_map/ppermute | solution.py:356
  16.0 2.5 %collective-permute-start.11 = (bf16[48,1024]{1,0:T(8,128)(2,1)S(1)}, bf16[48,1024]{1,0:T(8,128)(2,1)S(1)}, u32[]{:S(2)}, u32[]{:S(2)}) collective-permute-start(bf16[48,1024]{1,0:T(8,128)(2,1)S(1)} %collective-permute-done.5.refs_1_), channel_id=1, source_target_pairs={{0,2},{2,0},{4,6},{6,4},{8,10},{10,8},{12,14},{14,12},{16,18},{18,... | collective-permute-start | bytes 294920 | tf_op jit(solution)/shard_map/ppermute | solution.py:356
  16.5 14.4 %collective-permute-start.1 = (bf16[128,2048]{1,0:T(8,128)(2,1)S(1)}, bf16[128,2048]{1,0:T(8,128)(2,1)S(1)}, u32[]{:S(2)}, u32[]{:S(2)}) collective-permute-start(bf16[128,2048]{1,0:T(8,128)(2,1)S(1)} %get-tuple-element.41), channel_id=1, source_target_pairs={{0,2},{2,0},{4,6},{6,4},{8,10},{10,8},{12,14},{14,12},{16,18},{18,... | collective-permute-start | bytes 1572872 | tf_op jit(solution)/shard_map/ppermute | solution.py:356
  16.5 5.2 %collective-permute-start.8 = (bf16[48,1024]{1,0:T(8,128)(2,1)S(1)}, bf16[48,1024]{1,0:T(8,128)(2,1)S(1)}, u32[]{:S(2)}, u32[]{:S(2)}) collective-permute-start(bf16[48,1024]{1,0:T(8,128)(2,1)S(1)} %collective-permute-done.4.refs_0_), channel_id=1, source_target_pairs={{0,8},{2,10},{4,0},{6,2},{8,16},{10,18},{12,4},{14,6},{16,24},{18,... | collective-permute-start | bytes 294920 | tf_op jit(solution)/shard_map/ppermute | solution.py:386
  18.1 4.9 %collective-permute-start.9 = (bf16[48,1024]{1,0:T(8,128)(2,1)S(1)}, bf16[48,1024]{1,0:T(8,128)(2,1)S(1)}, u32[]{:S(2)}, u32[]{:S(2)}) collective-permute-start(bf16[48,1024]{1,0:T(8,128)(2,1)S(1)} %collective-permute-done.5.refs_1_), channel_id=1, source_target_pairs={{0,4},{2,6},{4,12},{6,14},{8,0},{10,2},{12,20},{14,22},{16,8},{18,... | collective-permute-start | bytes 294920 | tf_op jit(solution)/shard_map/ppermute | solution.py:387
  23.0 2.1 %collective-permute-start.14 = (bf16[48,1024]{1,0:T(8,128)(2,1)S(1)}, bf16[48,1024]{1,0:T(8,128)(2,1)S(1)}, u32[]{:S(2)}, u32[]{:S(2)}) collective-permute-start(bf16[48,1024]{1,0:T(8,128)(2,1)S(1)} %collective-permute-done.8.refs_0_), channel_id=1, source_target_pairs={{0,2},{2,0},{4,6},{6,4},{8,10},{10,8},{12,14},{14,12},{16,18},{18,... | collective-permute-start | bytes 294920 | tf_op jit(solution)/shard_map/ppermute | solution.py:356
  23.0 2.1 %collective-permute-start.15 = (bf16[48,1024]{1,0:T(8,128)(2,1)S(1)}, bf16[48,1024]{1,0:T(8,128)(2,1)S(1)}, u32[]{:S(2)}, u32[]{:S(2)}) collective-permute-start(bf16[48,1024]{1,0:T(8,128)(2,1)S(1)} %collective-permute-done.9.refs_1_), channel_id=1, source_target_pairs={{0,2},{2,0},{4,6},{6,4},{8,10},{10,8},{12,14},{14,12},{16,18},{18,... | collective-permute-start | bytes 294920 | tf_op jit(solution)/shard_map/ppermute | solution.py:356
  23.5 4.7 %collective-permute-start.12 = (bf16[48,1024]{1,0:T(8,128)(2,1)S(1)}, bf16[48,1024]{1,0:T(8,128)(2,1)S(1)}, u32[]{:S(2)}, u32[]{:S(2)}) collective-permute-start(bf16[48,1024]{1,0:T(8,128)(2,1)S(1)} %collective-permute-done.8.refs_0_), channel_id=1, source_target_pairs={{0,8},{2,10},{4,0},{6,2},{8,16},{10,18},{12,4},{14,6},{16,24},{18,... | collective-permute-start | bytes 294920 | tf_op jit(solution)/shard_map/ppermute | solution.py:386
  25.1 5.0 %collective-permute-start.13 = (bf16[48,1024]{1,0:T(8,128)(2,1)S(1)}, bf16[48,1024]{1,0:T(8,128)(2,1)S(1)}, u32[]{:S(2)}, u32[]{:S(2)}) collective-permute-start(bf16[48,1024]{1,0:T(8,128)(2,1)S(1)} %collective-permute-done.9.refs_1_), channel_id=1, source_target_pairs={{0,6},{2,4},{4,14},{6,12},{8,2},{10,0},{12,22},{14,20},{16,10},{18... | collective-permute-start | bytes 294920 | tf_op jit(solution)/shard_map/ppermute | solution.py:387
  38.1 1.6 %collective-permute-start.16 = (bf16[128,1024]{1,0:T(8,128)(2,1)S(1)}, bf16[128,1024]{1,0:T(8,128)(2,1)S(1)}, u32[]{:S(2)}, u32[]{:S(2)}) collective-permute-start(bf16[128,1024]{1,0:T(8,128)(2,1)S(1)} %get-tuple-element.72), channel_id=1, source_target_pairs={{0,2},{2,0},{4,6},{6,4},{8,10},{10,8},{12,14},{14,12},{16,18},{18,... | collective-permute-start | bytes 786440 | tf_op jit(solution)/shard_map/ppermute | solution.py:356
  39.7 8.4 %collective-permute-start.17 = (bf16[128,1024]{1,0:T(8,128)(2,1)S(1)}, bf16[128,1024]{1,0:T(8,128)(2,1)S(1)}, u32[]{:S(2)}, u32[]{:S(2)}) collective-permute-start(bf16[128,1024]{1,0:T(8,128)(2,1)S(1)} %add_convert_fusion.1), channel_id=1, source_target_pairs={{0,1},{1,0},{2,3},{3,2},{4,5},{5,4},{6,7},{7,6},{8,9},{9,8},{10,11... | collective-permute-start | bytes 786440 | tf_op jit(solution)/shard_map/ppermute | solution.py:403
